TPU v7x, 256 devices: a whole 4x4x8 slice. The times are simulated.
256 devices in a mesh: inst: 32 (over z_lo, y, x), tp: 8 (over z_hi, core).
Axes of the slice: x: 4, y: 4, z: 8 (z_hi: 4, z_lo: 2; z = z_hi * 2 + z_lo), core: 2. Of those that a mesh axis runs over, the one named last changes fastest.
Arguments:
- query_one: bfloat16 [1024, 64, 128], P('inst', 'tp'), may hold values from -32 to 32
- key_one: bfloat16 [1024, 8, 128], P('inst', 'tp'), may hold values from -6 to 6
- value_one: bfloat16 [1024, 8, 128], P('inst', 'tp'), may hold values from -6 to 6
- key_pages: bfloat16 [4096, 8, 64, 128], P('inst', 'tp'), may hold values from -32 to 32
- value_pages: bfloat16 [4096, 8, 64, 128], P('inst', 'tp'), may hold values from -6 to 6
- page_table: int32 [1024, 4], P('inst'), may hold values from 0 to 127, as said below
- lengths: int32 [1024], P('inst'), may hold values from 8 to 254, as said below
- dest_instance: int32 [1024], P('inst'), may hold values from 0 to 31, as said below
- dest_slot: int32 [1024], P('inst'), may hold values from 0 to 31, as said below
- query_two: bfloat16 [1024, 64, 128], P('inst', 'tp'), may hold values from -32 to 32
- key_two: bfloat16 [1024, 8, 128], P('inst', 'tp'), may hold values from -6 to 6
- value_two: bfloat16 [1024, 8, 128], P('inst', 'tp'), may hold values from -6 to 6
- out_weight: bfloat16 [8192, 4096], P('tp'), may hold values from -0.1875 to 0.1875
Outputs:
- out_one: bfloat16 [1024, 4096], P('inst')
- out_two: bfloat16 [1024, 4096], P('inst')
- key_cache: bfloat16 [4096, 8, 64, 128], P('inst', 'tp')
- value_cache: bfloat16 [4096, 8, 64, 128], P('inst', 'tp')
Inputs may be any that keep to these rules, and one draw needn't show every extreme that they name: `page_table`: the rows of one instance name each of its 128 pages exactly once. `lengths`: some request has exactly 254. `dest_instance`: the 32 requests of one instance go to 32 different instances, and every instance receives exactly 32 requests. `dest_slot`: the requests that reach one instance take its slots once each.
All inputs are finite; a program needn't handle non-finite values.
Results may differ from a plain program's by a relative error of at most 0.022.
Values may be sent and summed in bfloat16 or wider, within the bound.
A program may use at most 64 MiB of HBM per device.

v0:
```python
import jax
import jax.numpy as jnp
from jax import lax
from jax.sharding import PartitionSpec as P

NEG = -1e30


def put_token(pages, token, position):
    rows = jnp.arange(pages.shape[0], dtype=jnp.int32)
    size = pages.shape[3]
    return pages.at[rows, position // size, :, position % size, :].set(token)


def attend(query, pages_k, pages_v, count):
    slots, heads, width = query.shape
    kv_heads = pages_k.shape[2]
    group = heads // kv_heads
    span = pages_k.shape[1] * pages_k.shape[3]
    grouped = query.reshape(slots, kv_heads, group, width)
    scores = jnp.einsum("skgd,spktd->skgpt", grouped, pages_k, preferred_element_type=jnp.float32)
    scores = scores.reshape(slots, kv_heads, group, span) * width ** (-0.5)
    live = jnp.arange(span, dtype=jnp.int32)[None, :] < count[:, None]
    live = live[:, None, None, :]
    scores = jnp.where(live, scores, NEG)
    top = jnp.max(scores, axis=-1, keepdims=True)
    expo = jnp.where(live, jnp.exp(scores - top), 0.0)
    weights = (expo / jnp.sum(expo, axis=-1, keepdims=True)).astype(jnp.bfloat16)
    weights = weights.reshape(slots, kv_heads, group, pages_k.shape[1], pages_k.shape[3])
    mixed = jnp.einsum("skgpt,spktd->skgd", weights, pages_v, preferred_element_type=jnp.float32)
    return mixed.astype(jnp.bfloat16).reshape(slots, heads * width)


def shards(
    query_one,
    key_one,
    value_one,
    key_pages,
    value_pages,
    page_table,
    lengths,
    dest_instance,
    dest_slot,
    query_two,
    key_two,
    value_two,
    out_weight,
):
    slots = lengths.shape[0]
    rows = jnp.arange(slots, dtype=jnp.int32)
    request_k = key_pages[page_table]
    request_v = value_pages[page_table]
    written_k = put_token(request_k, key_one, lengths)
    written_v = put_token(request_v, value_one, lengths)
    first = attend(query_one, written_k, written_v, lengths + 1)
    partial_one = jnp.dot(first, out_weight, preferred_element_type=jnp.float32)
    summed_one = lax.psum(partial_one.astype(jnp.bfloat16), "tp")
    count = lax.axis_size("inst")
    targets = jnp.arange(count, dtype=jnp.int32)
    chosen = dest_instance[None, :] == targets[:, None]
    source_row = jnp.sum(jnp.where(chosen, rows[None, :], 0), axis=1)
    present = jnp.any(chosen, axis=1)
    header = jnp.stack([jnp.where(present, dest_slot[source_row], -1), lengths[source_row]], axis=1)
    arrived_k, arrived_v, info = (
        lax.all_to_all(written_k[source_row], "inst", split_axis=0, concat_axis=0, tiled=True),
        lax.all_to_all(written_v[source_row], "inst", split_axis=0, concat_axis=0, tiled=True),
        lax.all_to_all(header, "inst", split_axis=0, concat_axis=0, tiled=True),
    )
    owner = jnp.sum(jnp.where(info[None, :, 0] == rows[:, None], targets[None, :], 0), axis=1)
    moved_k = arrived_k[owner]
    moved_v = arrived_v[owner]
    moved_lengths = info[owner, 1]
    moved_k = put_token(moved_k, key_two, moved_lengths + 1)
    moved_v = put_token(moved_v, value_two, moved_lengths + 1)
    second = attend(query_two, moved_k, moved_v, moved_lengths + 2)
    partial_two = jnp.dot(second, out_weight, preferred_element_type=jnp.float32)
    summed_two = lax.psum(partial_two.astype(jnp.bfloat16), "tp")
    pages_per = moved_k.shape[1]
    key_cache = moved_k.reshape(
        slots * pages_per, moved_k.shape[2], moved_k.shape[3], moved_k.shape[4]
    )
    value_cache = moved_v.reshape(
        slots * pages_per, moved_v.shape[2], moved_v.shape[3], moved_v.shape[4]
    )
    return (summed_one, summed_two, key_cache, value_cache)


def solution(mesh):
    return jax.shard_map(
        shards,
        mesh=mesh,
        in_specs=(
            P("inst", "tp", None),
            P("inst", "tp", None),
            P("inst", "tp", None),
            P("inst", "tp", None, None),
            P("inst", "tp", None, None),
            P("inst", None),
            P("inst"),
            P("inst"),
            P("inst"),
            P("inst", "tp", None),
            P("inst", "tp", None),
            P("inst", "tp", None),
            P("tp", None),
        ),
        out_specs=(
            P("inst", None),
            P("inst", None),
            P("inst", "tp", None, None),
            P("inst", "tp", None, None),
        ),
        check_vma=False,
    )
```

profile of v0, /device:TPU:8, one launch (start us, length us, event | category | flops | bytes accessed | tf_op | source)
XLA Modules:
  0.0 204.2 jit_solution(9042070977191796189)
XLA Ops:
  7.2 0.0 copy-start
  7.2 0.9 select_reduce_fusion.1
  8.1 0.8 fusion.22
  8.9 1.4 gather_fusion.3
  10.2 1.4 gather_fusion.2
  11.6 0.7 copy.25
  12.3 8.9 %all-to-all-start = ((s32[32,1,2]{2,1,0:T(1,128)}), s32[32,1,2]{2,1,0:T(1,128)S(1)}, u32[]{:S(2)}, u32[]{:S(2)}) async-start(s32[32,1,2]{2,1,0:T(1,128)} %copy.25), calls=%async_computation | async-start | bytes 32768 | tf_op jit(solution)/shard_map/all_to_all | solution.py:67
  21.2 0.7 fusion.31
  21.9 0.7 compare_select_fusion
  22.6 0.1 copy.24
  22.7 0.1 reshape.309
  22.8 0.0 copy-done
  22.8 0.0 copy-start.5
  22.8 2.1 %gather_fusion = bf16[128,64,128]{2,1,0:T(8,128)(2,1)} fusion(bf16[128,64,128]{2,1,0:T(8,128)(2,1)S(1)} %bitcast.117, s32[1024]{0:T(1024)S(1)} %pad_clamp_fusion.2), kind=kCustom, calls=%fused_computation | custom fusion | bytes 4194816 | tf_op jit(solution)/shard_map/gather | solution.py:51
  25.0 0.0 copy-done.5
  25.0 4.0 %scatter_fusion = bf16[32,4,64,128]{3,2,1,0:T(8,128)(2,1)} fusion(bf16[32,4,64,128]{3,2,1,0:T(8,128)(2,1)} %bitcast.122, s32[32]{0:T(128)S(1)} %fusion.31, bf16[32,128]{1,0:T(8,128)(2,1)S(1)} %bitcast.131), kind=kCustom, calls=%fused_computation.9 | custom fusion | bytes 24960 | tf_op jit(solution)/shard_map/scatter | solution.py:12
  29.0 3.7 %gather_fusion.5 = bf16[32,4,64,128]{3,2,1,0:T(8,128)(2,1)} fusion(bf16[32,4,64,128]{3,2,1,0:T(8,128)(2,1)} %scatter_fusion, s32[1024]{0:T(1024)S(1)} %pad_clamp_fusion.1), kind=kCustom, calls=%fused_computation.5 | custom fusion | bytes 4194432 | tf_op jit(solution)/shard_map/gather | solution.py:65
  32.7 0.0 all-to-all-done
  32.7 8.4 %all-to-all-start.1 = ((bf16[32,4,1,64,128]{4,3,1,2,0:T(8,128)(2,1)}), bf16[32,4,1,64,128]{4,3,1,2,0:T(8,128)(2,1)}, u32[]{:S(2)}, u32[]{:S(2)}) async-start(bf16[32,4,1,64,128]{4,3,1,2,0:T(8,128)(2,1)} %bitcast.126), calls=%async_computation.1 | async-start | bytes 4194304 | tf_op jit(solution)/shard_map/all_to_all | solution.py:65
  41.1 0.0 copy-start.6
  41.1 3.7 %gather_fusion.1 = bf16[128,64,128]{2,1,0:T(8,128)(2,1)} fusion(bf16[128,64,128]{2,1,0:T(8,128)(2,1)} %bitcast.128, s32[1024]{0:T(1024)S(1)} %pad_clamp_fusion.2), kind=kCustom, calls=%fused_computation.1 | custom fusion | bytes 4194816 | tf_op jit(solution)/shard_map/gather | solution.py:52
  44.8 0.0 copy-done.6
  44.8 4.0 %scatter_fusion.1 = bf16[32,4,64,128]{3,2,1,0:T(8,128)(2,1)} fusion(bf16[32,4,64,128]{3,2,1,0:T(8,128)(2,1)} %bitcast.123, s32[32]{0:T(128)S(1)} %fusion.31, bf16[32,128]{1,0:T(8,128)(2,1)S(1)} %bitcast.132), kind=kCustom, calls=%fused_computation.10 | custom fusion | bytes 24960 | tf_op jit(solution)/shard_map/scatter | solution.py:12
  48.9 3.7 %gather_fusion.7 = bf16[32,4,64,128]{3,2,1,0:T(8,128)(2,1)} fusion(bf16[32,4,64,128]{3,2,1,0:T(8,128)(2,1)} %scatter_fusion.1, s32[1024]{0:T(1024)S(1)} %pad_clamp_fusion.1), kind=kCustom, calls=%fused_computation.7 | custom fusion | bytes 4194432 | tf_op jit(solution)/shard_map/gather | solution.py:66
  52.6 14.9 %all-to-all-done.1 = bf16[32,4,1,64,128]{4,3,1,2,0:T(8,128)(2,1)} async-done(((bf16[32,4,1,64,128]{4,3,1,2,0:T(8,128)(2,1)}), bf16[32,4,1,64,128]{4,3,1,2,0:T(8,128)(2,1)}, u32[]{:S(2)}, u32[]{:S(2)}) %all-to-all-start.1) | async-done | bytes 2097184 | tf_op jit(solution)/shard_map/all_to_all | solution.py:65
  67.5 0.0 copy-start.1
  67.5 0.0 copy-start.3
  67.5 7.0 %all-to-all-start.2 = ((bf16[32,4,1,64,128]{4,3,1,2,0:T(8,128)(2,1)}), bf16[32,4,1,64,128]{4,3,1,2,0:T(8,128)(2,1)}, u32[]{:S(2)}, u32[]{:S(2)}) async-start(bf16[32,4,1,64,128]{4,3,1,2,0:T(8,128)(2,1)} %bitcast.125), calls=%async_computation.2 | async-start | bytes 4194304 | tf_op jit(solution)/shard_map/all_to_all | solution.py:66
  74.4 0.2 all-reduce.4.cloned.1.call-start
  74.7 0.0 copy-done.1
  74.7 0.1 copy.26
  74.8 0.1 select_reduce_fusion
  74.9 0.8 gather_fusion.4
  75.7 0.1 broadcast_compare_fusion
  75.8 0.0 copy-done.3
  75.9 3.4 %fusion.36 = (f32[32,8]{1,0:T(8,128)S(1)}, f32[32,8,4,64]{3,1,2,0:T(8,128)S(1)}) fusion(bf16[32,4,64,128]{3,2,1,0:T(8,128)(2,1)} %scatter_fusion, bf16[32,8,128]{2,1,0:T(8,128)(2,1)S(1)} %copy-done.3, pred[32,4,64]{2,1,0:T(4,128)(4,1)S(1)} %get-tuple-element.15), kind=kOutput, calls=%fused_computation.101 | convolution fusion | flops 16973568 | bytes 2434048 | tf_op jit(solution)/shard_map/skgd,spktd->skgpt/dot_general | solution.py:21
  79.2 0.0 copy-start.7
  79.2 0.0 copy-start.4
  79.3 3.8 %gather_fusion.6 = bf16[32,4,64,128]{3,2,1,0:T(8,128)(2,1)} fusion(bf16[32,4,64,128]{3,2,1,0:T(8,128)(2,1)} %bitcast.24, s32[1024]{0:T(1024)S(1)} %pad_clamp_fusion), kind=kCustom, calls=%fused_computation.6 | custom fusion | bytes 4194432 | tf_op jit(solution)/shard_map/gather | solution.py:70
  83.0 0.0 copy-done.7
  83.0 4.0 %scatter_fusion.2 = bf16[32,4,64,128]{3,2,1,0:T(8,128)(2,1)} fusion(bf16[32,4,64,128]{3,2,1,0:T(8,128)(2,1)} %gather_fusion.6, s32[32]{0:T(128)S(1)} %fusion.32, bf16[32,128]{1,0:T(8,128)(2,1)S(1)} %bitcast.133), kind=kCustom, calls=%fused_computation.11 | custom fusion | bytes 24960 | tf_op jit(solution)/shard_map/scatter | solution.py:12
  87.0 0.0 copy-start.2
  87.0 0.0 copy-done.4
  87.0 3.5 %fusion.37 = (f32[32,8]{1,0:T(8,128)S(1)}, f32[32,8,4,64]{3,1,2,0:T(8,128)S(1)}) fusion(bf16[32,4,64,128]{3,2,1,0:T(8,128)(2,1)} %scatter_fusion.2, bf16[32,8,128]{2,1,0:T(8,128)(2,1)S(1)} %copy-done.4, pred[32,4,64]{2,1,0:T(4,128)(4,1)S(1)} %get-tuple-element.14), kind=kOutput, calls=%fused_computation.102 | convolution fusion | flops 16973568 | bytes 2434048 | tf_op jit(solution)/shard_map/skgd,spktd->skgpt/dot_general | solution.py:21
  90.6 0.4 fusion.6
  91.0 0.0 copy-done.2
  91.0 0.7 fusion.4
  91.7 9.8 %all-to-all-done.2 = bf16[32,4,1,64,128]{4,3,1,2,0:T(8,128)(2,1)} async-done(((bf16[32,4,1,64,128]{4,3,1,2,0:T(8,128)(2,1)}), bf16[32,4,1,64,128]{4,3,1,2,0:T(8,128)(2,1)}, u32[]{:S(2)}, u32[]{:S(2)}) %all-to-all-start.2) | async-done | bytes 2097184 | tf_op jit(solution)/shard_map/all_to_all | solution.py:66
  101.6 0.0 copy-start.8
  101.6 3.7 %gather_fusion.8 = bf16[32,4,64,128]{3,2,1,0:T(8,128)(2,1)} fusion(bf16[32,4,64,128]{3,2,1,0:T(8,128)(2,1)} %bitcast.33, s32[1024]{0:T(1024)S(1)} %pad_clamp_fusion), kind=kCustom, calls=%fused_computation.8 | custom fusion | bytes 4194432 | tf_op jit(solution)/shard_map/gather | solution.py:71
  105.3 0.0 copy-done.8
  105.3 4.0 %scatter_fusion.3 = bf16[32,4,64,128]{3,2,1,0:T(8,128)(2,1)} fusion(bf16[32,4,64,128]{3,2,1,0:T(8,128)(2,1)} %gather_fusion.8, s32[32]{0:T(128)S(1)} %fusion.32, bf16[32,128]{1,0:T(8,128)(2,1)S(1)} %bitcast.134), kind=kCustom, calls=%fused_computation.12 | custom fusion | bytes 24960 | tf_op jit(solution)/shard_map/scatter | solution.py:12
  109.3 0.0 slice-start
  109.3 2.4 %fusion.5 = bf16[32,8,128]{2,1,0:T(8,128)(2,1)S(1)} fusion(bf16[32,4,64,128]{3,2,1,0:T(8,128)(2,1)} %scatter_fusion.3, f32[32,8,4,64]{3,1,2,0:T(8,128)S(1)} %get-tuple-element.21, f32[32,8]{1,0:T(8,128)S(1)} %get-tuple-element.23, f32[32,8]{1,0:T(8,128)S(1)} %get-tuple-element.20, pred[32,4,64]{2,1,0:T(4,128)(4,1)S(1)} %get-tuple-element.14), kind=kOutput, calls=%fused_computation.24 | convolution fusion | flops 17072128 | bytes 2435072 | tf_op jit(solution)/shard_map/skgpt,spktd->skgd/dot_general | solution.py:30
  111.7 0.0 slice-start.1
  111.7 5.8 %convolution_convert_fusion = bf16[32,4096]{1,0:T(8,128)(2,1)} fusion(bf16[1024,4096]{1,0:T(8,128)(2,1)} %param.25, bf16[4,8,8,128]{3,2,1,0:T(8,128)(2,1)S(1)} %bitcast.130), kind=kOutput, calls=%fused_computation.13 | convolution fusion | flops 268566528 | bytes 8716288 | tf_op jit(solution)/shard_map/dot_general | solution.py:76
  117.5 0.0 slice-done
  117.5 0.0 slice-done.1
  117.5 2.3 %convolution_convert_fusion.1 = bf16[32,4096]{1,0:T(8,128)(2,1)} fusion(bf16[1024,4096]{1,0:T(8,128)(2,1)S(1)} %bitcast.121, bf16[4,8,8,128]{3,2,1,0:T(8,128)(2,1)S(1)} %bitcast.129), kind=kOutput, calls=%fused_computation.14 | convolution fusion | flops 268566528 | bytes 8716288 | tf_op jit(solution)/shard_map/dot_general | solution.py:56
  119.8 0.0 all-reduce.4.cloned.1.call-update
  119.8 74.2 %all-reduce.4.cloned.1.call-done = (bf16[32,4096]{1,0:T(8,128)(2,1)}, bf16[32,4096]{1,0:T(8,128)(2,1)}) async-done(((bf16[32,4096]{1,0:T(8,128)(2,1)}, bf16[32,4096]{1,0:T(8,128)(2,1)}), (bf16[32,4096]{1,0:T(8,128)(2,1)}, bf16[32,4096]{1,0:T(8,128)(2,1)})) %all-reduce.4.cloned.1.call-update) | async-done | bytes 524304 | tf_op jit(solution)/shard_map/psum | solution.py:57
  194.0 1.7 copy.49
  195.7 1.7 copy.50
  (13 shorter events, 0.1 us)
Async XLA Ops:
  7.2 15.6 %copy-start = (bf16[128,1,64,128]{3,2,1,0:T(8,128)(2,1)S(1)}, bf16[128,1,64,128]{3,2,1,0:T(8,128)(2,1)}, u32[]{:S(2)}) copy-start(bf16[128,1,64,128]{3,2,1,0:T(8,128)(2,1)} %param.16) | copy-start | bytes 6291460
  12.3 20.4 %all-to-all-start = ((s32[32,1,2]{2,1,0:T(1,128)}), s32[32,1,2]{2,1,0:T(1,128)S(1)}, u32[]{:S(2)}, u32[]{:S(2)}) async-start(s32[32,1,2]{2,1,0:T(1,128)} %copy.25), calls=%async_computation | async-start | bytes 32768 | tf_op jit(solution)/shard_map/all_to_all | solution.py:67
  22.8 2.1 %copy-start.5 = (bf16[32,1,128]{2,0,1:T(8,128)(2,1)S(1)}, bf16[32,1,128]{2,0,1:T(8,128)(2,1)}, u32[]{:S(2)}) copy-start(bf16[32,1,128]{2,0,1:T(8,128)(2,1)} %param.14) | copy-start | bytes 24580
  32.7 34.7 %all-to-all-start.1 = ((bf16[32,4,1,64,128]{4,3,1,2,0:T(8,128)(2,1)}), bf16[32,4,1,64,128]{4,3,1,2,0:T(8,128)(2,1)}, u32[]{:S(2)}, u32[]{:S(2)}) async-start(bf16[32,4,1,64,128]{4,3,1,2,0:T(8,128)(2,1)} %bitcast.126), calls=%async_computation.1 | async-start | bytes 4194304 | tf_op jit(solution)/shard_map/all_to_all | solution.py:65
  41.1 3.7 %copy-start.6 = (bf16[32,1,128]{2,0,1:T(8,128)(2,1)S(1)}, bf16[32,1,128]{2,0,1:T(8,128)(2,1)}, u32[]{:S(2)}) copy-start(bf16[32,1,128]{2,0,1:T(8,128)(2,1)} %param.15) | copy-start | bytes 24580
  67.5 7.2 %copy-start.1 = (s32[32]{0:T(128)S(1)}, s32[32]{0:T(128)}, u32[]{:S(2)}) copy-start(s32[32]{0:T(128)} %param.19) | copy-start | bytes 388
  67.5 8.4 %copy-start.3 = (bf16[32,8,128]{2,1,0:T(8,128)(2,1)S(1)}, bf16[32,8,128]{2,1,0:T(8,128)(2,1)}, u32[]{:S(2)}) copy-start(bf16[32,8,128]{2,1,0:T(8,128)(2,1)} %param.13) | copy-start | bytes 196612
  67.5 34.1 %all-to-all-start.2 = ((bf16[32,4,1,64,128]{4,3,1,2,0:T(8,128)(2,1)}), bf16[32,4,1,64,128]{4,3,1,2,0:T(8,128)(2,1)}, u32[]{:S(2)}, u32[]{:S(2)}) async-start(bf16[32,4,1,64,128]{4,3,1,2,0:T(8,128)(2,1)} %bitcast.125), calls=%async_computation.2 | async-start | bytes 4194304 | tf_op jit(solution)/shard_map/all_to_all | solution.py:66
  74.4 119.6 %all-reduce.4.cloned.1.call-start = ((), (), s32[]{:S(2)}) async-start(), calls=%async_computation.3 | async-start | bytes 1048576 | tf_op jit(solution)/shard_map/psum | solution.py:57
  79.2 3.8 %copy-start.7 = (bf16[32,1,128]{2,0,1:T(8,128)(2,1)S(1)}, bf16[32,1,128]{2,0,1:T(8,128)(2,1)}, u32[]{:S(2)}) copy-start(bf16[32,1,128]{2,0,1:T(8,128)(2,1)} %param.23) | copy-start | bytes 24580
  79.2 7.8 %copy-start.4 = (bf16[32,8,128]{2,1,0:T(8,128)(2,1)S(1)}, bf16[32,8,128]{2,1,0:T(8,128)(2,1)}, u32[]{:S(2)}) copy-start(bf16[32,8,128]{2,1,0:T(8,128)(2,1)} %param.22) | copy-start | bytes 196612
  87.0 4.0 %copy-start.2 = (bf16[32,4,64,128]{3,2,1,0:T(8,128)(2,1)S(1)}, bf16[32,4,64,128]{3,2,1,0:T(8,128)(2,1)}, u32[]{:S(2)}) copy-start(bf16[32,4,64,128]{3,2,1,0:T(8,128)(2,1)} %scatter_fusion.1) | copy-start | bytes 6291460
  101.6 3.7 %copy-start.8 = (bf16[32,1,128]{2,0,1:T(8,128)(2,1)S(1)}, bf16[32,1,128]{2,0,1:T(8,128)(2,1)}, u32[]{:S(2)}) copy-start(bf16[32,1,128]{2,0,1:T(8,128)(2,1)} %param.24) | copy-start | bytes 24580
  109.3 8.2 %slice-start = ((s8[8388608]{0:T(1024)(128)(4,1)}), s8[4194304]{0:T(1024)(128)(4,1)S(1)}, s32[]{:S(2)}) async-start(s8[8388608]{0:T(1024)(128)(4,1)} %bitcast.120), calls=%async_computation.4 | async-start | bytes 8388608
  111.7 5.8 %slice-start.1 = ((s8[8388608]{0:T(1024)(128)(4,1)}), s8[4194304]{0:T(1024)(128)(4,1)S(1)}, s32[]{:S(2)}) async-start(s8[8388608]{0:T(1024)(128)(4,1)} %bitcast.120), calls=%async_computation.5 | async-start | bytes 8388608
Sparse Core Ops, SparseCore 0:
  119.9 74.0 all-reduce.3
where the time goes:
time: 205 us; the launch traced here: 204 us
  waiting for transfers between devices  98.9 us (48%)
  local copies, waits for them, and re-layouts  44.7 us (22%)
  starting transfers between devices  24.4 us (12%)
  matrix products  18.1 us (9%)
  between operations  14.2 us (7%)
  other arithmetic  3.83 us (2%)
    psum x1, waiting for transfers between devices, shards(): summed_one = lax.psum(partial_one.astype(jnp.bfloat16), 'tp')  74.2 us
    scatter x4, local copies, waits for them, and re-layouts, put_token(): return pages.at[rows, position // size, :, position % size, :].set(token)  16.1 us
    all_to_all x1, waiting for transfers between devices, shards(): lax.all_to_all(written_k[source_row], 'inst', split_axis=0, concat_axis=0...  14.9 us
    all_to_all x1, waiting for transfers between devices, shards(): lax.all_to_all(written_v[source_row], 'inst', split_axis=0, concat_axis=0...  9.81 us
    all_to_all x1, starting transfers between devices, shards(): lax.all_to_all(header, 'inst', split_axis=0, concat_axis=0, tiled=True)  8.89 us
    all_to_all x1, starting transfers between devices, shards(): lax.all_to_all(written_k[source_row], 'inst', split_axis=0, concat_axis=0...  8.38 us
    all_to_all x1, starting transfers between devices, shards(): lax.all_to_all(written_v[source_row], 'inst', split_axis=0, concat_axis=0...  6.96 us
    dot_general x2, matrix products, attend(): jnp.einsum('skgd,spktd->skgpt', grouped, pages_k, preferred_element_type=...  6.94 us
  transfers between devices with their start and end apart: 4, of which 3 were waited for; matrix products, arithmetic and copies ran while one was open for 20% of the time, Pallas kernels for 0%

commit v1 on v0

v1 whole, which is shorter than its diff:
```python
import jax
import jax.numpy as jnp
from jax import lax
from jax.experimental import pallas as pl
from jax.experimental.pallas import tpu as pltpu
from jax.sharding import PartitionSpec as P

MESH = pl.DeviceIdType.MESH
NEG = -1e30
N = 32
TP = 8
ZH = 4
PR = 4
PAGE = 64
SPAN = PR * PAGE
HD = 128
G = 8
CH = 512
WINDOW = 8
BATCH = 4
F32 = jnp.float32
BF16 = jnp.bfloat16


def iota(shape, dim):
    return lax.broadcasted_iota(jnp.int32, shape, dim)


def attend(queries, keys, values, counts):
    scores = [
        lax.dot_general(q, k, (((1,), (1,)), ((), ())), preferred_element_type=F32)
        for q, k in zip(queries, keys)
    ]
    live = jnp.concatenate([iota((G, SPAN), 1) < n for n in counts], axis=0)
    scores = jnp.concatenate(scores, axis=0) * HD ** (-0.5)
    scores = jnp.where(live, scores, NEG)
    top = jnp.max(scores, axis=-1, keepdims=True)
    expo = jnp.where(live, jnp.exp(scores - top), 0.0)
    weights = (expo / jnp.sum(expo, axis=-1, keepdims=True)).astype(BF16)
    return [
        jnp.dot(weights[i * G : (i + 1) * G], v, preferred_element_type=F32)
        for i, v in enumerate(values)
    ]


def put_token(page, token, first_row, position):
    return jnp.where(iota(page.shape, 0) + first_row == position, token, page)


def exchange_kernel(
    pt, dest_s, len_s, dest_v, slot_v, len_v, q1, k1, v1, q2, k2, v2, kp, vp, w_hbm,
    moved, hdr_r, out1, out2,
    kpv, vpv, w, send, tab_v, tab_s, hdr_s, hdr_rs, rep_s, rep_r, o1, os, orr, lhs,
    own, pa_s, pa_r, pb_s, pb_r,
    lsem, hs, hr, rs, rr, ss, sr, bs, br, psem,
):
    me, tp = lax.axis_index("inst"), lax.axis_index("tp")
    x, y, zl = me % 4, (me // 4) % 4, me // 16
    core, zh = tp % 2, tp // 2

    def load(src, dst, i):
        return pltpu.make_async_copy(src, dst, lsem.at[i])

    load(kp, kpv, 0).start()
    load(vp, vpv, 1).start()
    load(w_hbm, w, 2).start()

    barrier = pltpu.get_barrier_semaphore()

    def greet_inst(i, c):
        pl.semaphore_signal(barrier, inc=1, device_id={"inst": (me + i) % N}, device_id_type=MESH)
        return c

    def greet_tp(i, c):
        pl.semaphore_signal(barrier, inc=1, device_id={"tp": (tp + i) % TP}, device_id_type=MESH)
        return c

    lax.fori_loop(1, N, greet_inst, 0)
    lax.fori_loop(1, TP, greet_tp, 0)

    here = dest_v[...] == iota((N, N), 0)
    row = jnp.max(jnp.where(here, iota((N, N), 1), 0), axis=1, keepdims=True)
    length = jnp.max(jnp.where(here, len_v[...], 0), axis=1, keepdims=True)
    slot = jnp.max(jnp.where(here, slot_v[...], 0), axis=1, keepdims=True)
    lane = iota((N, 128), 1)
    tab_v[...] = jnp.where(lane < 32, row, jnp.where(lane < 64, length, slot))
    to_scalar = load(tab_v, tab_s, 3)
    to_scalar.start()
    to_scalar.wait()

    def header(t, c):
        hdr_s[t] = jnp.where(iota((1, 128), 1) < 64, tab_s[t, 64], tab_s[t, 32])
        return c

    lax.fori_loop(0, N, header, 0)

    def remote(src, dst, send_sem, recv_sem, device):
        return pltpu.make_async_remote_copy(
            src_ref=src, dst_ref=dst, send_sem=send_sem, recv_sem=recv_sem,
            device_id=device, device_id_type=MESH,
        )

    def each_other(body):
        def step(i, c):
            body((me + i) % N)
            return c

        lax.fori_loop(1, N, step, 0)

    def send_header(t):
        return remote(hdr_s.at[t], hdr_r.at[me], hs.at[t], hr.at[me], {"inst": t})

    def wait_header(t):
        return remote(hdr_s.at[t], hdr_r.at[t], hs.at[t], hr.at[t], {"inst": t})

    pl.semaphore_wait(barrier, N + TP - 2)
    each_other(lambda t: send_header(t).start())
    hdr_r[me] = hdr_s[me]

    def offset(k):
        i, j = k % 4, k // 4
        dx, dy, dz = i, (i + j) % 4, (i // 2 + j // 4) % 2
        return dx, dy, dz

    def target(k, sign):
        dx, dy, dz = offset(k)
        turn = sign * (1 - 2 * core)
        return (((zl + dz) % 2) * 4 + (y + 4 + turn * dy) % 4) * 4 + (x + 4 + turn * dx) % 4

    def gather(t):
        r, n = tab_s[t, 0], tab_s[t, 32]
        for which, (pages, token) in enumerate(((kpv, k1), (vpv, v1))):
            for p in range(PR):
                page = put_token(pages[pt[r, p]], token[r], p * PAGE, n)
                send[t, which, p * PAGE : (p + 1) * PAGE] = page

    def block_out(k):
        t = target(k, 1)
        return remote(send.at[t], moved.at[me], bs.at[t], br.at[me], {"inst": t})

    def block_in(k):
        s = target(k, -1)
        return remote(send.at[s], moved.at[s], bs.at[s], br.at[s], {"inst": s}), s

    load(kp, kpv, 0).wait()
    load(vp, vpv, 1).wait()

    def first_blocks(k, c):
        gather(target(k, 1))
        block_out(k).start()
        return c

    def later_blocks(k, c):
        gather(target(k, 1))
        return c

    lax.fori_loop(1, 1 + WINDOW, first_blocks, 0)
    lax.fori_loop(1 + WINDOW, N, later_blocks, 0)
    gather(me)

    def pump(k):
        block_out(k - WINDOW).wait_send()
        block_out(k).start()

    def pumps(lo, hi):
        def step(k, c):
            pump(k)
            return c

        lax.fori_loop(lo, hi, step, 0)

    def attend_one(g, c):
        rows = [g * BATCH + i for i in range(BATCH)]
        at = [dest_s[r] for r in rows]
        res = attend(
            [q1[r] for r in rows], [send[t, 0] for t in at], [send[t, 1] for t in at],
            [len_s[r] + 1 for r in rows],
        )
        for r, one in zip(rows, res):
            o1[pl.ds(pl.multiple_of(r * G, G), G), :] = one
        return c

    lax.fori_loop(0, 4, attend_one, 0)
    pumps(9, 11)

    each_other(lambda t: wait_header(t).wait())
    fetch = load(hdr_r, hdr_rs, 4)
    fetch.start()
    fetch.wait()

    def reply(s, c):
        j = hdr_rs[s, 0, 0]
        token = jnp.where(iota((G, HD), 0) == 0, k2[j].astype(F32), v2[j].astype(F32))
        rep_s[s] = jnp.concatenate([q2[j].astype(F32), token], axis=0).astype(BF16)
        return c

    lax.fori_loop(0, N, reply, 0)
    each_other(lambda s: remote(rep_s.at[s], rep_r.at[me], rs.at[s], rr.at[me], {"inst": s}).start())
    rep_r[me] = rep_s[me]
    pumps(11, 13)
    lax.fori_loop(4, 8, attend_one, 0)
    pumps(13, 15)

    def project(side, chunk):
        at = pl.multiple_of(side * (ZH * CH) + chunk * CH, CH)
        return jnp.dot(lhs[...], w[:, pl.ds(at, CH)], preferred_element_type=F32)

    def heads_side_by_side(ref):
        parts = [ref[pl.ds(h, N, stride=G), :] for h in range(G)]
        return jnp.concatenate(parts, axis=1).astype(BF16)

    other = {"tp": zh * 2 + 1 - core}

    def sum_a(i):
        def away(h, c):
            pa_s[i, h] = project(1 - core, h).astype(BF16)
            return c

        lax.fori_loop(0, ZH, away, 0)
        remote(pa_s.at[i], pa_r.at[i], psem.at[i, 0], psem.at[i, 1], other).start()

        def keep(h, c):
            own[i, h] = project(core, h)
            return c

        lax.fori_loop(0, ZH, keep, 0)

    def part_b(i, d):
        h = (zh + d) % ZH
        return remote(pb_s.at[i, h], pb_r.at[i, zh], psem.at[i, 2 + d], psem.at[i, 6 + zh], {"tp": h * 2 + core}), h

    def sum_b(i):
        remote(pa_s.at[i], pa_r.at[i], psem.at[i, 0], psem.at[i, 1], other).wait()
        for h in range(ZH):
            both = own[i, h] + pa_r[i, h].astype(F32)
            own[i, h] = both
            pb_s[i, h] = both.astype(BF16)
        for d in range(1, ZH):
            part_b(i, d)[0].start()

    outs = (out1, out2)

    def chunk_to(i, h, device, send_at, recv_at):
        at = core * ZH + h
        return remote(outs[i].at[at], outs[i].at[at], psem.at[i, send_at], psem.at[i, recv_at], device)

    def sum_c(i):
        total = own[i, zh]
        for d in range(1, ZH):
            part, h = part_b(i, d)
            part.wait_send()
            remote(pb_s.at[i, h], pb_r.at[i, h], psem.at[i, 2 + d], psem.at[i, 6 + h], {"tp": h * 2 + core}).wait_recv()
            total = total + pb_r[i, h].astype(F32)
        outs[i][core * ZH + zh] = total.astype(BF16)
        for d in range(1, ZH):
            chunk_to(i, zh, {"tp": ((zh + d) % ZH) * 2 + core}, 10 + d, 14 + zh).start()
        chunk_to(i, zh, other, 18 + zh, 22 + zh).start()

    def sum_d(i):
        for d in range(1, ZH):
            h = (zh + d) % ZH
            chunk_to(i, h, {"tp": h * 2 + core}, 10 + d, 14 + h).wait()
            chunk_to(i, h, other, 18 + h, 22 + h).start()

    def sum_end(i):
        for h in range(ZH):
            at = (1 - core) * ZH + h
            chunk_to(i, h, other, 18 + h, 22 + h).wait_send()
            remote(outs[i].at[at], outs[i].at[at], psem.at[i, 18 + h], psem.at[i, 22 + h], other).wait_recv()

    load(w_hbm, w, 2).wait()
    lhs[...] = heads_side_by_side(o1)
    sum_a(0)
    pumps(15, 17)

    each_other(lambda t: remote(rep_s.at[t], rep_r.at[t], rs.at[t], rr.at[t], {"inst": t}).wait())

    def attend_two(g):
        ts = [g * BATCH + i for i in range(BATCH)]
        tiles = [rep_r[t].astype(F32) for t in ts]
        at = [tab_s[t, 32] + 1 for t in ts]
        keys = [put_token(send[t, 0], m[G : G + 1].astype(BF16), 0, n) for t, m, n in zip(ts, tiles, at)]
        values = [put_token(send[t, 1], m[G + 1 : G + 2].astype(BF16), 0, n) for t, m, n in zip(ts, tiles, at)]
        res = attend([m[:G].astype(BF16) for m in tiles], keys, values, [n + 1 for n in at])
        for t, one in zip(ts, res):
            os[pl.ds(pl.multiple_of(t * G, G), G), :] = one.astype(BF16).astype(F32)

    def rows_of(ref, s):
        return ref.at[pl.ds(pl.multiple_of(s * G, G), G), :]

    def result_out(t):
        return remote(rows_of(os, t), rows_of(orr, me), ss.at[t], sr.at[me], {"inst": t})

    def result_in(s):
        return remote(rows_of(os, s), rows_of(orr, s), ss.at[s], sr.at[s], {"inst": s})

    def half_two(lo, hi):
        def step(g, c):
            attend_two(g)
            for i in range(BATCH):
                t = g * BATCH + i

                @pl.when(t != me)
                def _():
                    result_out(t).start()

            return c

        lax.fori_loop(lo, hi, step, 0)

    half_two(0, 4)
    sum_b(0)
    pumps(17, 20)
    half_two(4, 8)
    orr[pl.ds(pl.multiple_of(me * G, G), G), :] = os[pl.ds(pl.multiple_of(me * G, G), G), :]
    pumps(20, 22)
    sum_c(0)

    each_other(lambda s: result_in(s).wait())

    def slot_row(s, acc):
        return jnp.where(iota((1, 128), 1) == s, hdr_rs[s, 0, 0], acc)

    slots = lax.fori_loop(0, N, slot_row, jnp.zeros((1, 128), jnp.int32))
    pick = jnp.where(slots[:, :N] == iota((N, N), 0), 1.0, 0.0).astype(BF16)
    lhs[...] = jnp.dot(pick, heads_side_by_side(orr), preferred_element_type=F32).astype(BF16)
    sum_a(1)
    sum_d(0)
    pumps(22, 24)
    sum_b(1)
    pumps(24, 28)
    sum_c(1)
    sum_end(0)
    pumps(28, 32)
    sum_d(1)

    def finish(s):
        n, j = hdr_rs[s, 0, 64] + 1, hdr_rs[s, 0, 0]
        for which, token in enumerate((k2, v2)):
            moved[s, which] = put_token(moved[s, which], token[j], 0, n)

    for which in range(2):
        moved[me, which] = send[me, which]
    finish(me)

    def arrive(k, c):
        copy, s = block_in(k)
        copy.wait_recv()
        finish(s)
        return c

    lax.fori_loop(1, N, arrive, 0)

    def sent(k, c):
        block_out(k).wait_send()
        return c

    lax.fori_loop(N - WINDOW, N, sent, 0)
    sum_end(1)


def place_kernel(hdr, moved, part1, part2, out1, out2, key_cache, value_cache, sems):
    caches = (key_cache, value_cache)

    def put(s, c):
        for which, cache in enumerate(caches):
            pltpu.make_async_copy(moved.at[s, which], cache.at[hdr[s, 0, 0]], sems.at[which]).start()
        return c

    lax.fori_loop(0, N, put, 0)
    for part, out in ((part1, out1), (part2, out2)):
        for c in range(TP):
            out[:, c * CH : (c + 1) * CH] = part[c]
    for which, cache in enumerate(caches):
        pltpu.make_async_copy(moved.at[:, which], cache, sems.at[which]).wait()


def shards(
    query_one, key_one, value_one, key_pages, value_pages, page_table, lengths,
    dest_instance, dest_slot, query_two, key_two, value_two, out_weight,
):
    vmem = pl.BlockSpec(memory_space=pltpu.VMEM)
    smem = pl.BlockSpec(memory_space=pltpu.SMEM)
    hbm = pl.BlockSpec(memory_space=pl.ANY)
    columns = out_weight.shape[1]
    pool = key_pages.shape[0]
    dma = pltpu.SemaphoreType.DMA
    moved, hdr, part1, part2 = pl.pallas_call(
        exchange_kernel,
        out_shape=(
            jax.ShapeDtypeStruct((N, 2, SPAN, HD), BF16),
            jax.ShapeDtypeStruct((N, 1, 128), jnp.int32),
            jax.ShapeDtypeStruct((TP, N, CH), BF16),
            jax.ShapeDtypeStruct((TP, N, CH), BF16),
        ),
        in_specs=[smem] * 3 + [vmem] * 9 + [hbm] * 3,
        out_specs=(vmem, vmem, vmem, vmem),
        scratch_shapes=[
            pltpu.VMEM((pool, PAGE, HD), BF16),
            pltpu.VMEM((pool, PAGE, HD), BF16),
            pltpu.VMEM((G * HD, columns), BF16),
            pltpu.VMEM((N, 2, SPAN, HD), BF16),
            pltpu.VMEM((N, 128), jnp.int32),
            pltpu.SMEM((N, 128), jnp.int32),
            pltpu.VMEM((N, 1, 128), jnp.int32),
            pltpu.SMEM((N, 1, 128), jnp.int32),
            pltpu.VMEM((N, 2 * G, HD), BF16),
            pltpu.VMEM((N, 2 * G, HD), BF16),
            pltpu.VMEM((N * G, HD), F32),
            pltpu.VMEM((N * G, HD), F32),
            pltpu.VMEM((N * G, HD), F32),
            pltpu.VMEM((N, G * HD), BF16),
            pltpu.VMEM((2, ZH, N, CH), F32),
            pltpu.VMEM((2, ZH, N, CH), BF16),
            pltpu.VMEM((2, ZH, N, CH), BF16),
            pltpu.VMEM((2, ZH, N, CH), BF16),
            pltpu.VMEM((2, ZH, N, CH), BF16),
            dma((5,)),
            dma((N,)), dma((N,)), dma((N,)), dma((N,)), dma((N,)), dma((N,)), dma((N,)), dma((N,)),
            dma((2, 26)),
        ],
        compiler_params=pltpu.CompilerParams(
            collective_id=0, has_side_effects=True, vmem_limit_bytes=48 << 20
        ),
        name="exchange",
    )(
        page_table, dest_instance, lengths,
        dest_instance.reshape(1, N), dest_slot.reshape(1, N), lengths.reshape(1, N),
        query_one, key_one, value_one, query_two, key_two, value_two,
        key_pages.reshape(pool, PAGE, HD), value_pages.reshape(pool, PAGE, HD), out_weight,
    )
    out1, out2, key_cache, value_cache = pl.pallas_call(
        place_kernel,
        out_shape=(
            jax.ShapeDtypeStruct((N, columns), BF16),
            jax.ShapeDtypeStruct((N, columns), BF16),
            jax.ShapeDtypeStruct((N, SPAN, HD), BF16),
            jax.ShapeDtypeStruct((N, SPAN, HD), BF16),
        ),
        in_specs=[smem, hbm, vmem, vmem],
        out_specs=(vmem, vmem, hbm, hbm),
        scratch_shapes=[dma((2,))],
        compiler_params=pltpu.CompilerParams(vmem_limit_bytes=48 << 20),
        name="place",
    )(hdr, moved, part1, part2)
    shape = (N * PR, 1, PAGE, HD)
    return out1, out2, key_cache.reshape(shape), value_cache.reshape(shape)


def solution(mesh):
    return jax.shard_map(
        shards,
        mesh=mesh,
        in_specs=(
            P("inst", "tp", None),
            P("inst", "tp", None),
            P("inst", "tp", None),
            P("inst", "tp", None, None),
            P("inst", "tp", None, None),
            P("inst", None),
            P("inst"),
            P("inst"),
            P("inst"),
            P("inst", "tp", None),
            P("inst", "tp", None),
            P("inst", "tp", None),
            P("tp", None),
        ),
        out_specs=(
            P("inst", None),
            P("inst", None),
            P("inst", "tp", None, None),
            P("inst", "tp", None, None),
        ),
        check_vma=False,
    )
```

time: 205 us -> 97.2 us (0.47)
  waiting for transfers between devices: 98.9 us -> 0 us
  Pallas kernels: 0 us -> 83.4 us
  local copies, waits for them, and re-layouts: 44.7 us -> 12.6 us
  starting transfers between devices: 24.4 us -> 0 us
  matrix products: 18.1 us -> 0 us
  between operations: 14.2 us -> 0.67 us
  other arithmetic: 3.83 us -> 0 us
    pallas_call x0 -> x2, Pallas kernels: none -> 83.4 us  [the longest x1 79.8 us: shards(): pl.pallas_call(exchange_kernel, out_shape=(jax.ShapeDtypeStruct((N, 2, SP...]
    psum x1 -> x0, waiting for transfers between devices: 74.2 us -> none  [shards(): summed_one = lax.psum(partial_one.astype(jnp.bfloat16), 'tp')]
    all_to_all x3 -> x0, waiting for transfers between devices: 24.7 us -> none  [the longest x1 14.9 us: shards(): lax.all_to_all(written_k[source_row], 'inst', split_axis=0, concat_axis=0...]
    gather x9 -> x0, local copies, waits for them, and re-layouts: 24.3 us -> none  [the longest x1 3.77 us: shards(): moved_k = arrived_k[owner]]
    all_to_all x3 -> x0, starting transfers between devices: 24.2 us -> none  [the longest x1 8.89 us: shards(): lax.all_to_all(header, 'inst', split_axis=0, concat_axis=0, tiled=True)]
    dot_general x6 -> x0, matrix products: 18.1 us -> none  [the longest x2 6.94 us: attend(): jnp.einsum('skgd,spktd->skgpt', grouped, pages_k, preferred_element_type=...]
    scatter x4 -> x0, local copies, waits for them, and re-layouts: 16.1 us -> none  [put_token(): return pages.at[rows, position // size, :, position % size, :].set(token)]
    unnamed x24 -> x21, local copies, waits for them, and re-layouts: 3.39 us -> 12.6 us
  transfers between devices with their start and end apart: 4 -> 0, of which waited for: 3 -> 0; matrix products, arithmetic and copies ran while one was open for 20% -> 0% of each run, Pallas kernels for 0% -> 0%
where the time goes in v1:
time: 97.2 us; the launch traced here: 96.7 us
  Pallas kernels  83.4 us (86%)
  local copies, waits for them, and re-layouts  12.6 us (13%)
    pallas_call x1, Pallas kernels, shards(): pl.pallas_call(exchange_kernel, out_shape=(jax.ShapeDtypeStruct((N, 2, SP...  79.8 us
    unnamed x21, local copies, waits for them, and re-layouts  12.6 us
    pallas_call x1, Pallas kernels, shards(): pl.pallas_call(place_kernel, out_shape=(jax.ShapeDtypeStruct((N, columns)...  3.57 us

profile of v1, /device:TPU:8, one launch (start us, length us, event | category | flops | bytes accessed | tf_op | source)
XLA Modules:
  0.0 96.7 jit_solution(6044021531920393760)
XLA Ops:
  0.6 0.7 copy.18.k1
  1.3 0.7 copy.19.v1
  2.1 0.8 copy.17.pt
  2.8 0.7 copy.20.k2
  3.5 0.7 copy.21.v2
  4.3 0.0 copy-start.1
  4.3 1.6 %copy-done.1 = bf16[128,1,64,128]{3,2,1,0:T(8,128)(2,1)S(1)} copy-done((bf16[128,1,64,128]{3,2,1,0:T(8,128)(2,1)S(1)}, bf16[128,1,64,128]{3,2,1,0:T(8,128)(2,1)}, u32[]{:S(2)}) %copy-start.1) | copy-done | bytes 2097176
  5.8 0.0 copy-start.2
  5.9 1.6 %copy-done.2 = bf16[128,1,64,128]{3,2,1,0:T(8,128)(2,1)S(1)} copy-done((bf16[128,1,64,128]{3,2,1,0:T(8,128)(2,1)S(1)}, bf16[128,1,64,128]{3,2,1,0:T(8,128)(2,1)}, u32[]{:S(2)}) %copy-start.2) | copy-done | bytes 2097176
  7.4 0.0 copy-start.3
  7.4 0.8 copy-done.3
  8.3 0.0 copy-start.4
  8.3 0.8 copy-done.4
  9.1 0.0 copy-start.5
  9.1 0.7 copy-done.5
  9.8 0.0 copy-start.6
  9.8 0.7 copy-done.6
  10.4 0.0 copy-start.7
  10.4 0.7 copy-done.7
  11.1 79.8 %exchange.1 = (bf16[32,2,256,128]{3,2,1,0:T(8,128)(2,1)}, s32[32,1,128]{2,1,0:T(1,128)S(1)}, bf16[8,32,512]{2,1,0:T(8,128)(2,1)S(1)}, bf16[8,32,512]{2,1,0:T(8,128)(2,1)S(1)}) custom-call(s32[32,4]{1,0:T(8,128)S(1)} %copy.17.pt, s32[32]{0:T(128)S(1)} %copy-done.5, s32[32]{0:T(128)S(1)} %copy-done.6, s32[1,32]{1,0:T(1,128)S(1)} %bitcast.13, ...), custom_call_target="tpu_custom_call" | custom-call | tf_op jit(solution)/shard_map/exchange/pallas_call | solution.py:388
  90.9 0.0 copy-start
  90.9 2.2 %copy-done = bf16[32,2,256,128]{3,2,1,0:T(8,128)(2,1)S(1)} copy-done((bf16[32,2,256,128]{3,2,1,0:T(8,128)(2,1)S(1)}, bf16[32,2,256,128]{3,2,1,0:T(8,128)(2,1)}, u32[]{:S(2)}) %copy-start) | copy-done | bytes 4194328
  93.1 3.6 %place.1 = (bf16[32,4096]{1,0:T(8,128)(2,1)}, bf16[32,4096]{1,0:T(8,128)(2,1)}, bf16[32,256,128]{2,1,0:T(8,128)(2,1)}, bf16[32,256,128]{2,1,0:T(8,128)(2,1)}) custom-call(s32[32,1,128]{2,1,0:T(1,128)S(1)} %get-tuple-element.12.hdr, bf16[32,2,256,128]{3,2,1,0:T(8,128)(2,1)S(1)} %copy-done, bf16[8,32,512]{2,1,0:T(8,128)(2,1)S(1)} %get-tuple-element.14.part1, ...), custom_call_target="tpu_custom_call" | custom-call | tf_op jit(solution)/shard_map/place/pallas_call | solution.py:432
Async XLA Ops:
  4.3 1.6 %copy-start.1 = (bf16[128,1,64,128]{3,2,1,0:T(8,128)(2,1)S(1)}, bf16[128,1,64,128]{3,2,1,0:T(8,128)(2,1)}, u32[]{:S(2)}) copy-start(bf16[128,1,64,128]{3,2,1,0:T(8,128)(2,1)} %param.16) | copy-start | bytes 6291460
  5.8 1.6 %copy-start.2 = (bf16[128,1,64,128]{3,2,1,0:T(8,128)(2,1)S(1)}, bf16[128,1,64,128]{3,2,1,0:T(8,128)(2,1)}, u32[]{:S(2)}) copy-start(bf16[128,1,64,128]{3,2,1,0:T(8,128)(2,1)} %param.17) | copy-start | bytes 6291460
  7.4 0.8 copy-start.3
  8.3 0.8 copy-start.4
  9.1 0.7 copy-start.5
  9.8 0.7 copy-start.6
  10.4 0.7 copy-start.7
  90.9 2.2 %copy-start = (bf16[32,2,256,128]{3,2,1,0:T(8,128)(2,1)S(1)}, bf16[32,2,256,128]{3,2,1,0:T(8,128)(2,1)}, u32[]{:S(2)}) copy-start(bf16[32,2,256,128]{3,2,1,0:T(8,128)(2,1)} %get-tuple-element.13.moved) | copy-start | bytes 12582916

commit v2 on v1

--- a/solution.py
+++ b/solution.py
@@ -48,9 +48,9 @@
 
 
 def exchange_kernel(
-    pt, dest_s, len_s, dest_v, slot_v, len_v, q1, k1, v1, q2, k2, v2, kp, vp, w_hbm,
+    pt_hbm, dest_hbm, slot_hbm, len_hbm, q1_hbm, k1_hbm, v1_hbm, q2_hbm, k2_hbm, v2_hbm, kp, vp, w_hbm,
     moved, hdr_r, out1, out2,
-    kpv, vpv, w, send, tab_v, tab_s, hdr_s, hdr_rs, rep_s, rep_r, o1, os, orr, lhs,
+    pt, dest_s, len_s, dest_v, slot_v, len_v, q1, q2, tok_b, tok, kpv, vpv, w, send, tab_v, tab_s, hdr_s, hdr_rs, rep_s, rep_r, o1, os, orr, lhs,
     own, pa_s, pa_r, pb_s, pb_r,
     lsem, hs, hr, rs, rr, ss, sr, bs, br, psem,
 ):
@@ -61,8 +61,21 @@
     def load(src, dst, i):
         return pltpu.make_async_copy(src, dst, lsem.at[i])
 
+    small = [
+        load(src, dst, 5 + i)
+        for i, (src, dst) in enumerate((
+            (dest_hbm, dest_v), (slot_hbm, slot_v), (len_hbm, len_v), (pt_hbm, pt),
+            (dest_hbm, dest_s), (len_hbm, len_s),
+            (k1_hbm, tok_b.at[0]), (v1_hbm, tok_b.at[1]), (k2_hbm, tok_b.at[2]), (v2_hbm, tok_b.at[3]),
+            (q1_hbm, q1), (q2_hbm, q2),
+        ))
+    ]
+    for copy in small[:8]:
+        copy.start()
     load(kp, kpv, 0).start()
     load(vp, vpv, 1).start()
+    for copy in small[8:]:
+        copy.start()
     load(w_hbm, w, 2).start()
 
     barrier = pltpu.get_barrier_semaphore()
@@ -77,6 +90,9 @@
 
     lax.fori_loop(1, N, greet_inst, 0)
     lax.fori_loop(1, TP, greet_tp, 0)
+
+    for copy in small[:8]:
+        copy.wait()
 
     here = dest_v[...] == iota((N, N), 0)
     row = jnp.max(jnp.where(here, iota((N, N), 1), 0), axis=1, keepdims=True)
@@ -129,9 +145,10 @@
 
     def gather(t):
         r, n = tab_s[t, 0], tab_s[t, 32]
-        for which, (pages, token) in enumerate(((kpv, k1), (vpv, v1))):
+        for which, pages in enumerate((kpv, vpv)):
+            token = tok[which, pl.ds(r, 1), :].astype(BF16)
             for p in range(PR):
-                page = put_token(pages[pt[r, p]], token[r], p * PAGE, n)
+                page = put_token(pages[pt[p, r]], token, p * PAGE, n)
                 send[t, which, p * PAGE : (p + 1) * PAGE] = page
 
     def block_out(k):
@@ -142,6 +159,9 @@
         s = target(k, -1)
         return remote(send.at[s], moved.at[s], bs.at[s], br.at[s], {"inst": s}), s
 
+    for copy in small[8:]:
+        copy.wait()
+    tok[...] = tok_b[...].astype(F32)
     load(kp, kpv, 0).wait()
     load(vp, vpv, 1).wait()
 
@@ -171,10 +191,10 @@
 
     def attend_one(g, c):
         rows = [g * BATCH + i for i in range(BATCH)]
-        at = [dest_s[r] for r in rows]
+        at = [dest_s[0, r] for r in rows]
         res = attend(
             [q1[r] for r in rows], [send[t, 0] for t in at], [send[t, 1] for t in at],
-            [len_s[r] + 1 for r in rows],
+            [len_s[0, r] + 1 for r in rows],
         )
         for r, one in zip(rows, res):
             o1[pl.ds(pl.multiple_of(r * G, G), G), :] = one
@@ -190,7 +210,7 @@
 
     def reply(s, c):
         j = hdr_rs[s, 0, 0]
-        token = jnp.where(iota((G, HD), 0) == 0, k2[j].astype(F32), v2[j].astype(F32))
+        token = jnp.where(iota((G, HD), 0) == 0, tok[2, pl.ds(j, 1), :], tok[3, pl.ds(j, 1), :])
         rep_s[s] = jnp.concatenate([q2[j].astype(F32), token], axis=0).astype(BF16)
         return c
 
@@ -336,8 +356,9 @@
 
     def finish(s):
         n, j = hdr_rs[s, 0, 64] + 1, hdr_rs[s, 0, 0]
-        for which, token in enumerate((k2, v2)):
-            moved[s, which] = put_token(moved[s, which], token[j], 0, n)
+        for which in range(2):
+            token = tok[2 + which, pl.ds(j, 1), :].astype(BF16)
+            moved[s, which] = put_token(moved[s, which], token, 0, n)
 
     for which in range(2):
         moved[me, which] = send[me, which]
@@ -381,21 +402,31 @@
 ):
     vmem = pl.BlockSpec(memory_space=pltpu.VMEM)
     smem = pl.BlockSpec(memory_space=pltpu.SMEM)
-    hbm = pl.BlockSpec(memory_space=pl.ANY)
+    hbm = pl.BlockSpec(memory_space=pltpu.HBM)
     columns = out_weight.shape[1]
     pool = key_pages.shape[0]
     dma = pltpu.SemaphoreType.DMA
     moved, hdr, part1, part2 = pl.pallas_call(
         exchange_kernel,
         out_shape=(
-            jax.ShapeDtypeStruct((N, 2, SPAN, HD), BF16),
-            jax.ShapeDtypeStruct((N, 1, 128), jnp.int32),
-            jax.ShapeDtypeStruct((TP, N, CH), BF16),
-            jax.ShapeDtypeStruct((TP, N, CH), BF16),
+            pltpu.VMEM((N, 2, SPAN, HD), BF16),
+            pltpu.VMEM((N, 1, 128), jnp.int32),
+            pltpu.VMEM((TP, N, CH), BF16),
+            pltpu.VMEM((TP, N, CH), BF16),
         ),
-        in_specs=[smem] * 3 + [vmem] * 9 + [hbm] * 3,
+        in_specs=[hbm] * 13,
         out_specs=(vmem, vmem, vmem, vmem),
         scratch_shapes=[
+            pltpu.SMEM((PR, N), jnp.int32),
+            pltpu.SMEM((1, N), jnp.int32),
+            pltpu.SMEM((1, N), jnp.int32),
+            pltpu.VMEM((1, N), jnp.int32),
+            pltpu.VMEM((1, N), jnp.int32),
+            pltpu.VMEM((1, N), jnp.int32),
+            pltpu.VMEM((N, G, HD), BF16),
+            pltpu.VMEM((N, G, HD), BF16),
+            pltpu.VMEM((4, N, HD), BF16),
+            pltpu.VMEM((4, N, HD), F32),
             pltpu.VMEM((pool, PAGE, HD), BF16),
             pltpu.VMEM((pool, PAGE, HD), BF16),
             pltpu.VMEM((G * HD, columns), BF16),
@@ -415,18 +446,18 @@
             pltpu.VMEM((2, ZH, N, CH), BF16),
             pltpu.VMEM((2, ZH, N, CH), BF16),
             pltpu.VMEM((2, ZH, N, CH), BF16),
-            dma((5,)),
+            dma((17,)),
             dma((N,)), dma((N,)), dma((N,)), dma((N,)), dma((N,)), dma((N,)), dma((N,)), dma((N,)),
             dma((2, 26)),
         ],
         compiler_params=pltpu.CompilerParams(
-            collective_id=0, has_side_effects=True, vmem_limit_bytes=48 << 20
+            collective_id=0, has_side_effects=True, vmem_limit_bytes=59 << 20
         ),
         name="exchange",
     )(
-        page_table, dest_instance, lengths,
-        dest_instance.reshape(1, N), dest_slot.reshape(1, N), lengths.reshape(1, N),
-        query_one, key_one, value_one, query_two, key_two, value_two,
+        page_table.T, dest_instance.reshape(1, N), dest_slot.reshape(1, N), lengths.reshape(1, N),
+        query_one, key_one.reshape(N, HD), value_one.reshape(N, HD),
+        query_two, key_two.reshape(N, HD), value_two.reshape(N, HD),
         key_pages.reshape(pool, PAGE, HD), value_pages.reshape(pool, PAGE, HD), out_weight,
     )
     out1, out2, key_cache, value_cache = pl.pallas_call(
@@ -437,12 +468,12 @@
             jax.ShapeDtypeStruct((N, SPAN, HD), BF16),
             jax.ShapeDtypeStruct((N, SPAN, HD), BF16),
         ),
-        in_specs=[smem, hbm, vmem, vmem],
+        in_specs=[smem, vmem, vmem, vmem],
         out_specs=(vmem, vmem, hbm, hbm),
         scratch_shapes=[dma((2,))],
         compiler_params=pltpu.CompilerParams(vmem_limit_bytes=48 << 20),
         name="place",
-    )(hdr, moved, part1, part2)
+    )(hdr, *(pltpu.with_memory_space_constraint(a, pltpu.VMEM) for a in (moved, part1, part2)))
     shape = (N * PR, 1, PAGE, HD)
     return out1, out2, key_cache.reshape(shape), value_cache.reshape(shape)
 

time: 97.2 us -> 82 us (0.84)
  local copies, waits for them, and re-layouts: 12.6 us -> 0 us
  Pallas kernels: 83.4 us -> 80.5 us
    unnamed x21 -> x0, local copies, waits for them, and re-layouts: 12.6 us -> none
    pallas_call x1, Pallas kernels: 79.8 us -> 77 us  [shards(): pl.pallas_call(exchange_kernel, out_shape=(pltpu.VMEM((N, 2, SPAN, HD), B...]
where the time goes in v2:
time: 82 us; the launch traced here: 81.2 us
  Pallas kernels  80.5 us (98%)
    pallas_call x1, Pallas kernels, shards(): pl.pallas_call(exchange_kernel, out_shape=(pltpu.VMEM((N, 2, SPAN, HD), B...  77 us
    pallas_call x1, Pallas kernels, shards(): pl.pallas_call(place_kernel, out_shape=(jax.ShapeDtypeStruct((N, columns)...  3.57 us

profile of v2, /device:TPU:8, one launch (start us, length us, event | category | flops | bytes accessed | tf_op | source)
XLA Modules:
  0.0 81.2 jit_solution(3606904085467309705)
XLA Ops:
  0.6 77.0 %exchange.1 = (bf16[32,2,256,128]{3,2,1,0:T(8,128)(2,1)S(1)}, s32[32,1,128]{2,1,0:T(1,128)S(1)}, bf16[8,32,512]{2,1,0:T(8,128)(2,1)S(1)}, bf16[8,32,512]{2,1,0:T(8,128)(2,1)S(1)}) custom-call(s32[4,32]{1,0:T(4,128)} %bitcast.22, s32[1,32]{1,0:T(1,128)} %bitcast.23, s32[1,32]{1,0:T(1,128)} %bitcast.24, s32[1,32]{1,0:T(1,128)} %bitcast.25, ...), custom_call_target="tpu_custom_call" | custom-call | tf_op jit(solution)/shard_map/exchange/pallas_call | solution.py:409
  77.6 3.6 %place.1 = (bf16[32,4096]{1,0:T(8,128)(2,1)}, bf16[32,4096]{1,0:T(8,128)(2,1)}, bf16[32,256,128]{2,1,0:T(8,128)(2,1)}, bf16[32,256,128]{2,1,0:T(8,128)(2,1)}) custom-call(s32[32,1,128]{2,1,0:T(1,128)S(1)} %get-tuple-element.12.hdr, bf16[32,2,256,128]{3,2,1,0:T(8,128)(2,1)S(1)} %get-tuple-element.13.moved, bf16[8,32,512]{2,1,0:T(8,128)(2,1)S(1)} %get-tuple-element.14.part1, ...), custom_call_target="tpu_custom_call" | custom-call | tf_op jit(solution)/shard_map/place/pallas_call | solution.py:463

commit v3 on v2

--- a/solution.py
+++ b/solution.py
@@ -16,8 +16,11 @@
 HD = 128
 G = 8
 CH = 512
-WINDOW = 8
-BATCH = 4
+QUARTERS = 4
+HALF = SPAN // 2
+BATCH = 8
+PIECES = N * QUARTERS
+WINDOW = 14
 F32 = jnp.float32
 BF16 = jnp.bfloat16
 
@@ -149,77 +152,99 @@
             token = tok[which, pl.ds(r, 1), :].astype(BF16)
             for p in range(PR):
                 page = put_token(pages[pt[p, r]], token, p * PAGE, n)
-                send[t, which, p * PAGE : (p + 1) * PAGE] = page
-
-    def block_out(k):
+                at = p * PAGE % HALF
+                send[t, which * 2 + p * PAGE // HALF, at : at + PAGE] = page
+
+    def gathers(lo, hi):
+        def step(k, c):
+            gather(target(k, 1))
+            return c
+
+        lax.fori_loop(lo, hi, step, 0)
+
+    def piece(v):
+        k, quarter = v // (BATCH * QUARTERS) * BATCH + v % BATCH, v // BATCH % QUARTERS
         t = target(k, 1)
-        return remote(send.at[t], moved.at[me], bs.at[t], br.at[me], {"inst": t})
+        return k, remote(send.at[t, quarter], moved.at[me, quarter], bs.at[v % 16], br.at[me], {"inst": t})
+
+    def piece_start(v):
+        k, copy = piece(v)
+
+        @pl.when(k != 0)
+        def _():
+            copy.start()
+
+    def piece_sent(v):
+        k, copy = piece(v)
+
+        @pl.when(k != 0)
+        def _():
+            copy.wait_send()
+
+    def pumps(lo, hi):
+        def step(v, c):
+            piece_sent(v - WINDOW)
+            piece_start(v)
+            return c
+
+        lax.fori_loop(lo, hi, step, 0)
+
+    def cache_of(ref, t):
+        return [ref[t, 2 * which : 2 * which + 2].reshape(SPAN, HD) for which in range(2)]
 
     def block_in(k):
         s = target(k, -1)
-        return remote(send.at[s], moved.at[s], bs.at[s], br.at[s], {"inst": s}), s
+        return remote(send.at[s], moved.at[s], bs.at[0], br.at[s], {"inst": s}), s
 
     for copy in small[8:]:
         copy.wait()
     tok[...] = tok_b[...].astype(F32)
     load(kp, kpv, 0).wait()
     load(vp, vpv, 1).wait()
-
-    def first_blocks(k, c):
-        gather(target(k, 1))
-        block_out(k).start()
-        return c
-
-    def later_blocks(k, c):
-        gather(target(k, 1))
-        return c
-
-    lax.fori_loop(1, 1 + WINDOW, first_blocks, 0)
-    lax.fori_loop(1 + WINDOW, N, later_blocks, 0)
-    gather(me)
-
-    def pump(k):
-        block_out(k - WINDOW).wait_send()
-        block_out(k).start()
-
-    def pumps(lo, hi):
-        def step(k, c):
-            pump(k)
-            return c
-
-        lax.fori_loop(lo, hi, step, 0)
+    gathers(0, BATCH)
+
+    def begin(v, c):
+        piece_start(v)
+        return c
+
+    lax.fori_loop(0, WINDOW, begin, 0)
+    gathers(BATCH, 2 * BATCH)
+    pumps(14, 16)
+    gathers(2 * BATCH, N)
+    pumps(16, 18)
 
     def attend_one(g, c):
         rows = [g * BATCH + i for i in range(BATCH)]
-        at = [dest_s[0, r] for r in rows]
+        caches = [cache_of(send, dest_s[0, r]) for r in rows]
         res = attend(
-            [q1[r] for r in rows], [send[t, 0] for t in at], [send[t, 1] for t in at],
+            [q1[r] for r in rows], [k for k, _ in caches], [v for _, v in caches],
             [len_s[0, r] + 1 for r in rows],
         )
         for r, one in zip(rows, res):
             o1[pl.ds(pl.multiple_of(r * G, G), G), :] = one
-        return c
-
-    lax.fori_loop(0, 4, attend_one, 0)
-    pumps(9, 11)
+        pumps(18 + 2 * g, 20 + 2 * g)
+        return c
+
+    lax.fori_loop(0, N // BATCH, attend_one, 0)
 
     each_other(lambda t: wait_header(t).wait())
     fetch = load(hdr_r, hdr_rs, 4)
     fetch.start()
     fetch.wait()
 
-    def reply(s, c):
+    def reply(s):
         j = hdr_rs[s, 0, 0]
         token = jnp.where(iota((G, HD), 0) == 0, tok[2, pl.ds(j, 1), :], tok[3, pl.ds(j, 1), :])
         rep_s[s] = jnp.concatenate([q2[j].astype(F32), token], axis=0).astype(BF16)
-        return c
-
-    lax.fori_loop(0, N, reply, 0)
-    each_other(lambda s: remote(rep_s.at[s], rep_r.at[me], rs.at[s], rr.at[me], {"inst": s}).start())
+
+    def reply_to(s):
+        reply(s)
+        remote(rep_s.at[s], rep_r.at[me], rs.at[s], rr.at[me], {"inst": s}).start()
+
+    each_other(reply_to)
+    reply(me)
     rep_r[me] = rep_s[me]
-    pumps(11, 13)
-    lax.fori_loop(4, 8, attend_one, 0)
-    pumps(13, 15)
+    pumps(26, 32)
 
     def project(side, chunk):
         at = pl.multiple_of(side * (ZH * CH) + chunk * CH, CH)
@@ -231,9 +256,10 @@
 
     other = {"tp": zh * 2 + 1 - core}
 
-    def sum_a(i):
+    def sum_a(i, v):
         def away(h, c):
             pa_s[i, h] = project(1 - core, h).astype(BF16)
+            pumps(v + h, v + h + 1)
             return c
 
         lax.fori_loop(0, ZH, away, 0)
@@ -241,6 +267,7 @@
 
         def keep(h, c):
             own[i, h] = project(core, h)
+            pumps(v + ZH + h, v + ZH + h + 1)
             return c
 
         lax.fori_loop(0, ZH, keep, 0)
@@ -290,79 +317,77 @@
 
     load(w_hbm, w, 2).wait()
     lhs[...] = heads_side_by_side(o1)
-    sum_a(0)
-    pumps(15, 17)
+    sum_a(0, 32)
+    pumps(40, 44)
+    sum_b(0)
+    pumps(44, 54)
 
     each_other(lambda t: remote(rep_s.at[t], rep_r.at[t], rs.at[t], rr.at[t], {"inst": t}).wait())
 
-    def attend_two(g):
-        ts = [g * BATCH + i for i in range(BATCH)]
+    def result_out(t):
+        return remote(os.at[t], orr.at[me], ss.at[t], sr.at[me], {"inst": t})
+
+    def result_in(s):
+        return remote(os.at[s], orr.at[s], ss.at[s], sr.at[s], {"inst": s})
+
+    def attend_two(g, v, keep):
+        ts = [target(g * BATCH + i, 1) for i in range(BATCH)]
         tiles = [rep_r[t].astype(F32) for t in ts]
         at = [tab_s[t, 32] + 1 for t in ts]
-        keys = [put_token(send[t, 0], m[G : G + 1].astype(BF16), 0, n) for t, m, n in zip(ts, tiles, at)]
-        values = [put_token(send[t, 1], m[G + 1 : G + 2].astype(BF16), 0, n) for t, m, n in zip(ts, tiles, at)]
-        res = attend([m[:G].astype(BF16) for m in tiles], keys, values, [n + 1 for n in at])
+        caches = [
+            [put_token(c, m[G + i : G + i + 1].astype(BF16), 0, n) for i, c in enumerate(cache_of(send, t))]
+            for t, m, n in zip(ts, tiles, at)
+        ]
+        if keep:
+            for t, cache in zip(ts, caches):
+                for which, c in enumerate(cache):
+                    send[t, 2 * which : 2 * which + 2] = c.reshape(2, HALF, HD)
+        res = attend(
+            [m[:G].astype(BF16) for m in tiles], [k for k, _ in caches], [v for _, v in caches],
+            [n + 1 for n in at],
+        )
         for t, one in zip(ts, res):
-            os[pl.ds(pl.multiple_of(t * G, G), G), :] = one.astype(BF16).astype(F32)
-
-    def rows_of(ref, s):
-        return ref.at[pl.ds(pl.multiple_of(s * G, G), G), :]
-
-    def result_out(t):
-        return remote(rows_of(os, t), rows_of(orr, me), ss.at[t], sr.at[me], {"inst": t})
-
-    def result_in(s):
-        return remote(rows_of(os, s), rows_of(orr, s), ss.at[s], sr.at[s], {"inst": s})
-
-    def half_two(lo, hi):
-        def step(g, c):
-            attend_two(g)
-            for i in range(BATCH):
-                t = g * BATCH + i
-
-                @pl.when(t != me)
-                def _():
-                    result_out(t).start()
-
-            return c
-
-        lax.fori_loop(lo, hi, step, 0)
-
-    half_two(0, 4)
-    sum_b(0)
-    pumps(17, 20)
-    half_two(4, 8)
-    orr[pl.ds(pl.multiple_of(me * G, G), G), :] = os[pl.ds(pl.multiple_of(me * G, G), G), :]
-    pumps(20, 22)
+            os[t] = one.astype(BF16)
+        for i, t in enumerate(ts):
+
+            @pl.when(g * BATCH + i != 0)
+            def _():
+                result_out(t).start()
+
+        pumps(v, v + 2)
+
+    def late_blocks(g, c):
+        attend_two(g, 54 + 2 * (g - 2), True)
+        return c
+
+    def early_blocks(g, c):
+        attend_two(g, 58 + 2 * g, False)
+        return c
+
+    lax.fori_loop(2, 4, late_blocks, 0)
+    lax.fori_loop(0, 2, early_blocks, 0)
+    orr[me] = os[me]
+    pumps(62, 70)
     sum_c(0)
+    pumps(70, 80)
 
     each_other(lambda s: result_in(s).wait())
+    o1[...] = orr[...].astype(F32).reshape(N * G, HD)
 
     def slot_row(s, acc):
         return jnp.where(iota((1, 128), 1) == s, hdr_rs[s, 0, 0], acc)
 
     slots = lax.fori_loop(0, N, slot_row, jnp.zeros((1, 128), jnp.int32))
     pick = jnp.where(slots[:, :N] == iota((N, N), 0), 1.0, 0.0).astype(BF16)
-    lhs[...] = jnp.dot(pick, heads_side_by_side(orr), preferred_element_type=F32).astype(BF16)
-    sum_a(1)
+    lhs[...] = jnp.dot(pick, heads_side_by_side(o1), preferred_element_type=F32).astype(BF16)
+    sum_a(1, 80)
     sum_d(0)
-    pumps(22, 24)
-    sum_b(1)
-    pumps(24, 28)
-    sum_c(1)
-    sum_end(0)
-    pumps(28, 32)
-    sum_d(1)
 
     def finish(s):
         n, j = hdr_rs[s, 0, 64] + 1, hdr_rs[s, 0, 0]
-        for which in range(2):
+        for which, page in enumerate(cache_of(moved, s)):
             token = tok[2 + which, pl.ds(j, 1), :].astype(BF16)
-            moved[s, which] = put_token(moved[s, which], token, 0, n)
-
-    for which in range(2):
-        moved[me, which] = send[me, which]
-    finish(me)
+            moved[s, 2 * which : 2 * which + 2] = put_token(page, token, 0, n).reshape(2, HALF, HD)
 
     def arrive(k, c):
         copy, s = block_in(k)
@@ -370,30 +395,53 @@
         finish(s)
         return c
 
-    lax.fori_loop(1, N, arrive, 0)
-
-    def sent(k, c):
-        block_out(k).wait_send()
-        return c
-
-    lax.fori_loop(N - WINDOW, N, sent, 0)
+    def arrive_late(k, c):
+        copy, _ = block_in(k)
+        copy.wait_recv()
+        return c
+
+    moved[me] = send[me]
+    finish(me)
+    lax.fori_loop(1, BATCH, arrive, 0)
+    pumps(88, 92)
+    sum_b(1)
+    pumps(92, 108)
+    sum_end(0)
+    sum_c(1)
+    lax.fori_loop(BATCH, 2 * BATCH, arrive, 0)
+    pumps(108, PIECES)
+    sum_d(1)
+
+    def sent(v, c):
+        piece_sent(v)
+        return c
+
+    lax.fori_loop(PIECES - WINDOW, PIECES, sent, 0)
+    lax.fori_loop(2 * BATCH, N, arrive_late, 0)
     sum_end(1)
 
 
 def place_kernel(hdr, moved, part1, part2, out1, out2, key_cache, value_cache, sems):
     caches = (key_cache, value_cache)
+    columns = [
+        pltpu.make_async_copy(part.at[c], out.at[:, pl.ds(c * CH, CH)], sems.at[2 + i * TP + c])
+        for i, (part, out) in enumerate(((part1, out1), (part2, out2)))
+        for c in range(TP)
+    ]
 
     def put(s, c):
         for which, cache in enumerate(caches):
-            pltpu.make_async_copy(moved.at[s, which], cache.at[hdr[s, 0, 0]], sems.at[which]).start()
-        return c
-
-    lax.fori_loop(0, N, put, 0)
-    for part, out in ((part1, out1), (part2, out2)):
-        for c in range(TP):
-            out[:, c * CH : (c + 1) * CH] = part[c]
+            half = moved.at[s, pl.ds(2 * which, 2)]
+            pltpu.make_async_copy(half, cache.at[hdr[s, 0, 0]], sems.at[which]).start()
+        return c
+
+    lax.fori_loop(0, N, put, 0, unroll=4)
+    for copy in columns:
+        copy.start()
+    for copy in columns:
+        copy.wait()
     for which, cache in enumerate(caches):
-        pltpu.make_async_copy(moved.at[:, which], cache, sems.at[which]).wait()
+        pltpu.make_async_copy(moved.at[:, pl.ds(2 * which, 2)], cache, sems.at[which]).wait()
 
 
 def shards(
@@ -409,7 +457,7 @@
     moved, hdr, part1, part2 = pl.pallas_call(
         exchange_kernel,
         out_shape=(
-            pltpu.VMEM((N, 2, SPAN, HD), BF16),
+            pltpu.VMEM((N, QUARTERS, HALF, HD), BF16),
             pltpu.VMEM((N, 1, 128), jnp.int32),
             pltpu.VMEM((TP, N, CH), BF16),
             pltpu.VMEM((TP, N, CH), BF16),
@@ -430,7 +478,7 @@
             pltpu.VMEM((pool, PAGE, HD), BF16),
             pltpu.VMEM((pool, PAGE, HD), BF16),
             pltpu.VMEM((G * HD, columns), BF16),
-            pltpu.VMEM((N, 2, SPAN, HD), BF16),
+            pltpu.VMEM((N, QUARTERS, HALF, HD), BF16),
             pltpu.VMEM((N, 128), jnp.int32),
             pltpu.SMEM((N, 128), jnp.int32),
             pltpu.VMEM((N, 1, 128), jnp.int32),
@@ -438,8 +486,8 @@
             pltpu.VMEM((N, 2 * G, HD), BF16),
             pltpu.VMEM((N, 2 * G, HD), BF16),
             pltpu.VMEM((N * G, HD), F32),
-            pltpu.VMEM((N * G, HD), F32),
-            pltpu.VMEM((N * G, HD), F32),
+            pltpu.VMEM((N, G, HD), BF16),
+            pltpu.VMEM((N, G, HD), BF16),
             pltpu.VMEM((N, G * HD), BF16),
             pltpu.VMEM((2, ZH, N, CH), F32),
             pltpu.VMEM((2, ZH, N, CH), BF16),
@@ -465,12 +513,12 @@
         out_shape=(
             jax.ShapeDtypeStruct((N, columns), BF16),
             jax.ShapeDtypeStruct((N, columns), BF16),
-            jax.ShapeDtypeStruct((N, SPAN, HD), BF16),
-            jax.ShapeDtypeStruct((N, SPAN, HD), BF16),
+            jax.ShapeDtypeStruct((N, 2, HALF, HD), BF16),
+            jax.ShapeDtypeStruct((N, 2, HALF, HD), BF16),
         ),
         in_specs=[smem, vmem, vmem, vmem],
-        out_specs=(vmem, vmem, hbm, hbm),
-        scratch_shapes=[dma((2,))],
+        out_specs=(hbm, hbm, hbm, hbm),
+        scratch_shapes=[dma((2 + 2 * TP,))],
         compiler_params=pltpu.CompilerParams(vmem_limit_bytes=48 << 20),
         name="place",
     )(hdr, *(pltpu.with_memory_space_constraint(a, pltpu.VMEM) for a in (moved, part1, part2)))

time: 82 us -> 78.8 us (0.961)
  Pallas kernels: 80.5 us -> 77.5 us
    pallas_call x1, Pallas kernels: 77 us -> 74.4 us  [shards(): pl.pallas_call(exchange_kernel, out_shape=(pltpu.VMEM((N, QUARTERS, HALF,...]
where the time goes in v3:
time: 78.8 us; the launch traced here: 78.1 us
  Pallas kernels  77.5 us (98%)
    pallas_call x1, Pallas kernels, shards(): pl.pallas_call(exchange_kernel, out_shape=(pltpu.VMEM((N, QUARTERS, HALF,...  74.4 us
    pallas_call x1, Pallas kernels, shards(): pl.pallas_call(place_kernel, out_shape=(jax.ShapeDtypeStruct((N, columns)...  3.08 us

profile of v3, /device:TPU:8, one launch (start us, length us, event | category | flops | bytes accessed | tf_op | source)
XLA Modules:
  0.0 78.1 jit_solution(188431257543709579)
XLA Ops:
  0.6 74.4 %exchange.1 = (bf16[32,4,128,128]{3,2,1,0:T(8,128)(2,1)S(1)}, s32[32,1,128]{2,1,0:T(1,128)S(1)}, bf16[8,32,512]{2,1,0:T(8,128)(2,1)S(1)}, bf16[8,32,512]{2,1,0:T(8,128)(2,1)S(1)}) custom-call(s32[4,32]{1,0:T(4,128)} %bitcast.22, s32[1,32]{1,0:T(1,128)} %bitcast.23, s32[1,32]{1,0:T(1,128)} %bitcast.24, s32[1,32]{1,0:T(1,128)} %bitcast.25, ...), custom_call_target="tpu_custom_call" | custom-call | tf_op jit(solution)/shard_map/exchange/pallas_call | solution.py:457
  75.0 3.1 %place.1 = (bf16[32,4096]{1,0:T(8,128)(2,1)}, bf16[32,4096]{1,0:T(8,128)(2,1)}, bf16[32,2,128,128]{3,2,1,0:T(8,128)(2,1)}, bf16[32,2,128,128]{3,2,1,0:T(8,128)(2,1)}) custom-call(s32[32,1,128]{2,1,0:T(1,128)S(1)} %get-tuple-element.12.hdr, bf16[32,4,128,128]{3,2,1,0:T(8,128)(2,1)S(1)} %get-tuple-element.13.moved, ...), custom_call_target="tpu_custom_call" | custom-call | tf_op jit(solution)/shard_map/place/pallas_call | solution.py:511

commit v4 on v3

--- a/solution.py
+++ b/solution.py
@@ -52,8 +52,8 @@
 
 def exchange_kernel(
     pt_hbm, dest_hbm, slot_hbm, len_hbm, q1_hbm, k1_hbm, v1_hbm, q2_hbm, k2_hbm, v2_hbm, kp, vp, w_hbm,
-    moved, hdr_r, out1, out2,
-    pt, dest_s, len_s, dest_v, slot_v, len_v, q1, q2, tok_b, tok, kpv, vpv, w, send, tab_v, tab_s, hdr_s, hdr_rs, rep_s, rep_r, o1, os, orr, lhs,
+    moved, hdr_rs, out1, out2,
+    pt, dest_s, len_s, dest_v, slot_v, len_v, q1, q2, tok_b, tok, kpv, vpv, w, send, tab_v, tab_s, hdr_s, hdr_r, rep_s, rep_r, o1, os, orr, lhs,
     own, pa_s, pa_r, pb_s, pb_r,
     lsem, hs, hr, rs, rr, ss, sr, bs, br, psem,
 ):
@@ -458,12 +458,12 @@
         exchange_kernel,
         out_shape=(
             pltpu.VMEM((N, QUARTERS, HALF, HD), BF16),
-            pltpu.VMEM((N, 1, 128), jnp.int32),
+            pltpu.SMEM((N, 1, 128), jnp.int32),
             pltpu.VMEM((TP, N, CH), BF16),
             pltpu.VMEM((TP, N, CH), BF16),
         ),
         in_specs=[hbm] * 13,
-        out_specs=(vmem, vmem, vmem, vmem),
+        out_specs=(vmem, smem, vmem, vmem),
         scratch_shapes=[
             pltpu.SMEM((PR, N), jnp.int32),
             pltpu.SMEM((1, N), jnp.int32),
@@ -482,7 +482,7 @@
             pltpu.VMEM((N, 128), jnp.int32),
             pltpu.SMEM((N, 128), jnp.int32),
             pltpu.VMEM((N, 1, 128), jnp.int32),
-            pltpu.SMEM((N, 1, 128), jnp.int32),
+            pltpu.VMEM((N, 1, 128), jnp.int32),
             pltpu.VMEM((N, 2 * G, HD), BF16),
             pltpu.VMEM((N, 2 * G, HD), BF16),
             pltpu.VMEM((N * G, HD), F32),
@@ -521,7 +521,7 @@
         scratch_shapes=[dma((2 + 2 * TP,))],
         compiler_params=pltpu.CompilerParams(vmem_limit_bytes=48 << 20),
         name="place",
-    )(hdr, *(pltpu.with_memory_space_constraint(a, pltpu.VMEM) for a in (moved, part1, part2)))
+    )(pltpu.with_memory_space_constraint(hdr, pltpu.SMEM), *(pltpu.with_memory_space_constraint(a, pltpu.VMEM) for a in (moved, part1, part2)))
     shape = (N * PR, 1, PAGE, HD)
     return out1, out2, key_cache.reshape(shape), value_cache.reshape(shape)
 

time: 78.8 us -> 78 us (0.990)
  Pallas kernels: 77.5 us -> 76.7 us
    pallas_call x1, Pallas kernels: 3.08 us -> 2.27 us  [shards(): pl.pallas_call(place_kernel, out_shape=(jax.ShapeDtypeStruct((N, columns)...]
where the time goes in v4:
time: 78 us; the launch traced here: 77.3 us
  Pallas kernels  76.7 us (98%)
    pallas_call x1, Pallas kernels, shards(): pl.pallas_call(exchange_kernel, out_shape=(pltpu.VMEM((N, QUARTERS, HALF,...  74.4 us
    pallas_call x1, Pallas kernels, shards(): pl.pallas_call(place_kernel, out_shape=(jax.ShapeDtypeStruct((N, columns)...  2.27 us

profile of v4, /device:TPU:8, one launch (start us, length us, event | category | flops | bytes accessed | tf_op | source)
XLA Modules:
  0.0 77.3 jit_solution(5839528758071529105)
XLA Ops:
  0.6 74.4 %exchange.1 = (bf16[32,4,128,128]{3,2,1,0:T(8,128)(2,1)S(1)}, s32[32,1,128]{2,1,0:T(1,128)S(4)}, bf16[8,32,512]{2,1,0:T(8,128)(2,1)S(1)}, bf16[8,32,512]{2,1,0:T(8,128)(2,1)S(1)}) custom-call(s32[4,32]{1,0:T(4,128)} %bitcast.22, s32[1,32]{1,0:T(1,128)} %bitcast.23, s32[1,32]{1,0:T(1,128)} %bitcast.24, s32[1,32]{1,0:T(1,128)} %bitcast.25, ...), custom_call_target="tpu_custom_call" | custom-call | tf_op jit(solution)/shard_map/exchange/pallas_call | solution.py:457
  75.0 2.3 %place.1 = (bf16[32,4096]{1,0:T(8,128)(2,1)}, bf16[32,4096]{1,0:T(8,128)(2,1)}, bf16[32,2,128,128]{3,2,1,0:T(8,128)(2,1)}, bf16[32,2,128,128]{3,2,1,0:T(8,128)(2,1)}) custom-call(s32[32,1,128]{2,1,0:T(1,128)S(4)} %get-tuple-element.12.hdr, bf16[32,4,128,128]{3,2,1,0:T(8,128)(2,1)S(1)} %get-tuple-element.13.moved, ...), custom_call_target="tpu_custom_call" | custom-call | tf_op jit(solution)/shard_map/place/pallas_call | solution.py:511
